TPU v7x, 256 devices: a whole 4x4x8 slice. The times are simulated.
256 devices in a mesh: row: 8 (over z_lo, core), col: 32 (over z_hi, y, x).
Axes of the slice: x: 4, y: 4, z: 8 (z_hi: 2, z_lo: 4; z = z_hi * 4 + z_lo), core: 2. Of those that a mesh axis runs over, the one named last changes fastest.
Arguments:
- tokens: bfloat16 [1024, 16384], P('row', 'col'), may hold values from -6 to 6
- w_query: bfloat16 [16384, 8192], P('col', 'row'), may hold values from -0.078125 to 0.078125
- w_keyval: bfloat16 [16384, 1024], P('col', 'row'), may hold values from -0.078125 to 0.078125
- w_output: bfloat16 [8192, 16384], P('row', 'col'), may hold values from -0.0625 to 0.0625
Outputs:
- result: bfloat16 [1024, 16384], P('row', 'col')
All inputs are finite; a program needn't handle non-finite values.
Results may differ from a plain program's by a relative error of at most 0.02.
Values may be sent and summed in bfloat16 or wider, within the bound.
No kernel may reach another device: no remote copies, remote signals or barrier semaphores. Data moves between devices by JAX's collectives and lax.ppermute only.
A program may use at most 64 MiB of HBM per device.

v0:
```python
import math
import jax
import jax.numpy as jnp
from jax import lax
from jax.sharding import PartitionSpec as P

HQ = 64
KVH = 4
HD = 128


def angles(positions, width):
    half_width = width // 2
    frequency = 500000.0 ** (-(jnp.arange(half_width).astype(jnp.float32) * 2.0 / width))
    angle_v = positions[:, None] * frequency[None, :]
    return (jnp.cos(angle_v), jnp.sin(angle_v))


def rotate(values_in, cosine, sine_v):
    half_width = values_in.shape[-1] // 2
    lower_half = values_in[..., :half_width]
    upper_half = values_in[..., half_width:]
    return jnp.concatenate(
        [lower_half * cosine - upper_half * sine_v, upper_half * cosine + lower_half * sine_v], -1
    )


def shards(tokens, w_query, w_keyval, w_output):
    n_row = lax.axis_size("row")
    n_col = lax.axis_size("col")
    row_index = lax.axis_index("row")
    col_index = lax.axis_index("col")
    gathered = lax.all_gather(tokens, "row", axis=0, tiled=True)
    all_rows = gathered.shape[0]
    per_col = all_rows // n_col
    query_width = w_query.shape[1]
    keyval_width = w_keyval.shape[1]
    heads_local = query_width // HD
    heads_per_block = keyval_width // HD
    query_part = jnp.dot(gathered, w_query, preferred_element_type=jnp.float32)
    keyval_part = jnp.dot(gathered, w_keyval, preferred_element_type=jnp.float32)
    query_cols = lax.psum_scatter(query_part, "col", scatter_dimension=1, tiled=True)
    keyval_block = lax.psum_scatter(keyval_part, "col", scatter_dimension=0, tiled=True)
    query_local = lax.all_to_all(query_cols, "col", split_axis=0, concat_axis=1, tiled=True)
    keyval_all = lax.all_gather(
        keyval_block.astype(jnp.bfloat16), ("row", "col"), axis=0, tiled=True
    )
    keyval_heads = keyval_all.reshape(n_row, all_rows, heads_per_block, HD)
    pattern = "hrm,rtmd->htd"
    query_index = col_index * per_col + jnp.arange(per_col, dtype=jnp.int32)
    key_index = jnp.arange(all_rows, dtype=jnp.int32)
    query_cos, query_sin = angles(query_index.astype(jnp.float32), HD)
    key_cos, key_sin = angles(key_index.astype(jnp.float32), HD)
    query = rotate(
        query_local.reshape(per_col, heads_local, HD), query_cos[:, None, :], query_sin[:, None, :]
    ).astype(jnp.bfloat16)
    global_head = row_index * heads_local + jnp.arange(heads_local, dtype=jnp.int32)
    key_head = global_head // (HQ // KVH)
    block_head = (
        jnp.arange(n_row, dtype=jnp.int32)[:, None] * heads_per_block
        + jnp.arange(heads_per_block, dtype=jnp.int32)[None, :]
    )
    pick_keys = (block_head[None, :, :] == key_head[:, None, None]).astype(jnp.bfloat16)
    pick_values = (block_head[None, :, :] == (key_head + KVH)[:, None, None]).astype(jnp.bfloat16)
    keys_sel = jnp.einsum(pattern, pick_keys, keyval_heads, preferred_element_type=jnp.float32)
    keys = rotate(keys_sel, key_cos[None, :, :], key_sin[None, :, :]).astype(jnp.bfloat16)
    values = jnp.einsum(
        pattern, pick_values, keyval_heads, preferred_element_type=jnp.float32
    ).astype(jnp.bfloat16)
    score_scale = 1.0 / math.sqrt(HD)
    scores = (
        jnp.einsum("thd,hsd->hts", query, keys, preferred_element_type=jnp.float32) * score_scale
    )
    causal = (key_index[None, :] <= query_index[:, None])[None, :, :]
    weights_raw = jnp.where(causal, jnp.exp(jnp.where(causal, scores, 0.0)), 0.0)
    totals = jnp.sum(weights_raw, -1)
    weights_b = weights_raw.astype(jnp.bfloat16)
    heads_mixed = jnp.einsum("hts,hsd->thd", weights_b, values, preferred_element_type=jnp.float32)
    heads_mixed = heads_mixed / jnp.transpose(totals)[:, :, None]
    attended = heads_mixed.astype(jnp.bfloat16).reshape(per_col, query_width)
    partial_out = jnp.dot(
        lax.all_gather(attended, "col", axis=0, tiled=True),
        w_output,
        preferred_element_type=jnp.float32,
    )
    return lax.psum_scatter(
        partial_out.astype(jnp.bfloat16), "row", scatter_dimension=0, tiled=True
    )


def solution(mesh):
    return jax.shard_map(
        shards,
        mesh=mesh,
        in_specs=(P("row", "col"), P("col", "row"), P("col", "row"), P("row", "col")),
        out_specs=P("row", "col"),
        check_vma=False,
    )
```

profile of v0, /device:TPU:6, one launch (start us, length us, event | category | flops | bytes accessed | tf_op | source)
XLA Modules:
  0.0 1362.1 jit_solution(6192898784604710600)
XLA Ops:
  7.3 42.1 %all-gather.4.cloned.1.call-done = bf16[1024,512]{1,0:T(8,128)(2,1)} async-done(((bf16[128,512]{1,0:T(8,128)(2,1)}), bf16[1024,512]{1,0:T(8,128)(2,1)}) %all-gather.4.cloned.1.call-update) | async-done | bytes 1048592 | tf_op jit(solution)/shard_map/all_gather | solution.py:33
  49.4 2.6 fusion.45
  52.1 206.8 %reduce-scatter.4.cloned.1.call-done = f32[32,128]{1,0:T(8,128)} async-done(((f32[1024,128]{1,0:T(8,128)}), f32[32,128]{1,0:T(8,128)}) %reduce-scatter.4.cloned.1.call-update) | async-done | bytes 16400 | tf_op jit(solution)/shard_map/reduce_scatter | solution.py:43
  258.8 1.3 convert_element_type.55
  260.3 3.3 fusion.46
  263.8 1.9 multiply_cosine_fusion
  265.7 693.1 %all-gather.6.cloned.1.call-done = bf16[8192,128]{1,0:T(8,128)(2,1)} async-done(((bf16[32,128]{1,0:T(8,128)(2,1)}), bf16[8192,128]{1,0:T(8,128)(2,1)}) %all-gather.6.cloned.1.call-update) | async-done | bytes 2097168 | tf_op jit(solution)/shard_map/all_gather | solution.py:45
  958.8 2.9 fusion.4
  961.7 1.8 subtract_convert_fusion
  963.6 2.5 pad_maximum_fusion
  966.1 221.4 %reduce-scatter.6.cloned.1.call-done = f32[1024,32]{0,1:T(8,128)} async-done(((f32[1024,1024]{0,1:T(8,128)}), f32[1024,32]{0,1:T(8,128)}) %reduce-scatter.6.cloned.1.call-update) | async-done | bytes 131088 | tf_op jit(solution)/shard_map/reduce_scatter | solution.py:42
  1187.5 1.9 copy.22
  1189.4 1.9 reshape.298
  1191.4 21.2 %all-to-all-start = ((f32[32,1,1024]{2,1,0:T(1,128)}), f32[32,1,1024]{2,1,0:T(1,128)S(1)}, u32[]{:S(2)}, u32[]{:S(2)}) async-start(f32[32,1,1024]{2,1,0:T(1,128)} %reshape.298), calls=%async_computation.2 | async-start | bytes 262144 | tf_op jit(solution)/shard_map/all_to_all | solution.py:44
  1212.8 2.7 convolution_convert_fusion
  1215.5 8.1 all-to-all-done
  1224.1 0.9 reduce
  1225.1 1.0 reshape.299
  1226.0 2.1 copy.15
  1228.2 1.2 reshape.294
  1229.6 1.0 fusion.44
  1232.5 85.5 %all-gather.8.cloned.1.call-done = bf16[1024,1024]{1,0:T(8,128)(2,1)} async-done(((bf16[32,1024]{1,0:T(8,128)(2,1)}), bf16[1024,1024]{1,0:T(8,128)(2,1)}) %all-gather.8.cloned.1.call-update) | async-done | bytes 2097168 | tf_op jit(solution)/shard_map/all_gather | solution.py:82
  1318.0 3.8 convolution_convert_fusion.1
  1321.8 33.5 %reduce-scatter.8.cloned.1.call-done = bf16[128,512]{1,0:T(8,128)(2,1)} async-done(((bf16[1024,512]{1,0:T(8,128)(2,1)}), bf16[128,512]{1,0:T(8,128)(2,1)}) %reduce-scatter.8.cloned.1.call-update) | async-done | bytes 131088 | tf_op jit(solution)/shard_map/reduce_scatter | solution.py:86
  (35 shorter events, 3.9 us)
Async XLA Ops:
  6.5 253.7 %copy-start = (bf16[512,1024]{1,0:T(8,128)(2,1)S(1)}, bf16[512,1024]{1,0:T(8,128)(2,1)}, u32[]{:S(2)}) copy-start(bf16[512,1024]{1,0:T(8,128)(2,1)} %param.5) | copy-start | bytes 3145732
  6.5 42.9 %all-gather.4.cloned.1.call-start = ((), (), s32[]{:S(2)}) async-start(), calls=%async_computation.4 | async-start | bytes 1179648 | tf_op jit(solution)/shard_map/all_gather | solution.py:33
  7.3 251.6 %reduce-scatter.4.cloned.1.call-start = ((), (), s32[]{:S(2)}) async-start(), calls=%async_computation.5 | async-start | bytes 540672 | tf_op jit(solution)/shard_map/reduce_scatter | solution.py:43
  49.4 210.8 %copy-start.4 = (bf16[1024,512]{1,0:T(8,128)(2,1)S(1)}, bf16[1024,512]{1,0:T(8,128)(2,1)}, u32[]{:S(2)}) copy-start(bf16[1024,512]{1,0:T(8,128)(2,1)} %all-gather.4.cloned.1.call-done) | copy-start | bytes 3145732
  52.0 906.8 %all-gather.6.cloned.1.call-start = ((), (), s32[]{:S(2)}) async-start(), calls=%async_computation.6 | async-start | bytes 2105344 | tf_op jit(solution)/shard_map/all_gather | solution.py:45
  260.2 927.3 %reduce-scatter.6.cloned.1.call-start = ((), (), s32[]{:S(2)}) async-start(), calls=%async_computation.7 | async-start | bytes 4325376 | tf_op jit(solution)/shard_map/reduce_scatter | solution.py:42
  963.6 249.3 %copy-start.1 = (bf16[8192,128]{1,0:T(8,128)(2,1)S(1)}, bf16[8192,128]{1,0:T(8,128)(2,1)}, u32[]{:S(2)}) copy-start(bf16[8192,128]{1,0:T(8,128)(2,1)} %all-gather.6.cloned.1.call-done) | copy-start | bytes 6291460
  1191.4 32.2 %all-to-all-start = ((f32[32,1,1024]{2,1,0:T(1,128)}), f32[32,1,1024]{2,1,0:T(1,128)S(1)}, u32[]{:S(2)}, u32[]{:S(2)}) async-start(f32[32,1,1024]{2,1,0:T(1,128)} %reshape.298), calls=%async_computation.2 | async-start | bytes 262144 | tf_op jit(solution)/shard_map/all_to_all | solution.py:44
  1212.6 105.4 %all-gather.8.cloned.1.call-start = ((), (), s32[]{:S(2)}) async-start(), calls=%async_computation.8 | async-start | bytes 2162688 | tf_op jit(solution)/shard_map/all_gather | solution.py:82
  1215.5 14.0 %copy-start.2 = (bf16[8,1024,128]{2,0,1:T(8,128)(2,1)S(1)}, bf16[8,1024,128]{2,0,1:T(8,128)(2,1)}, u32[]{:S(2)}) copy-start(bf16[8,1024,128]{2,0,1:T(8,128)(2,1)} %pad_maximum_fusion) | copy-start | bytes 6291460
  1229.5 1.6 copy-start.3
  1230.6 87.4 %copy-start.5 = (bf16[1024,512]{1,0:T(8,128)(2,1)S(1)}, bf16[1024,512]{1,0:T(8,128)(2,1)}, u32[]{:S(2)}) copy-start(bf16[1024,512]{1,0:T(8,128)(2,1)} %param.7) | copy-start | bytes 3145732
  1232.5 122.8 %reduce-scatter.8.cloned.1.call-start = ((), (), s32[]{:S(2)}) async-start(), calls=%async_computation.9 | async-start | bytes 1179648 | tf_op jit(solution)/shard_map/reduce_scatter | solution.py:86
Sparse Core Ops, SparseCore 0:
  9.1 40.2 all-gather.3
  52.1 206.6 reduce-scatter.3
  260.9 697.8 all-gather.5
  961.4 226.0 reduce-scatter.5
  1232.6 85.3 all-gather.7
  1321.9 33.2 reduce-scatter.7
where the time goes:
time: 1360 us
  waiting for transfers between devices  1290 us (95%)
  starting transfers between devices  21.6 us (2%)
  matrix products  16.9 us (1%)
  between operations  13.6 us (1%)
    all_gather x1, waiting for transfers between devices, shards(): lax.all_gather(keyval_block.astype(jnp.bfloat16), ('row', 'col'), axis=0,...  693 us
    reduce_scatter x1, waiting for transfers between devices, shards(): lax.psum_scatter(query_part, 'col', scatter_dimension=1, tiled=True)  221 us
    reduce_scatter x1, waiting for transfers between devices, shards(): lax.psum_scatter(keyval_part, 'col', scatter_dimension=0, tiled=True)  207 us
    all_gather x1, waiting for transfers between devices, shards(): lax.all_gather(attended, 'col', axis=0, tiled=True)  85.5 us
    all_gather x1, waiting for transfers between devices, shards(): gathered = lax.all_gather(tokens, 'row', axis=0, tiled=True)  42.1 us
    reduce_scatter x1, waiting for transfers between devices, shards(): lax.psum_scatter(partial_out.astype(jnp.bfloat16), 'row', scatter_dimensi...  33.5 us
  transfers between devices with their start and end apart: 7, of which 7 were waited for; matrix products, arithmetic and copies ran while one was open for 1% of the time, Pallas kernels for 0%

commit v1 on v0

--- a/solution.py
+++ b/solution.py
@@ -79,7 +79,9 @@
     heads_mixed = heads_mixed / jnp.transpose(totals)[:, :, None]
     attended = heads_mixed.astype(jnp.bfloat16).reshape(per_col, query_width)
     partial_out = jnp.dot(
-        lax.all_gather(attended, "col", axis=0, tiled=True),
+        jnp.concatenate(
+            lax.all_to_all(jnp.stack([attended] * lax.axis_size("col")), "col", 0, 0), axis=0
+        ),
         w_output,
         preferred_element_type=jnp.float32,
     )

time: 1360 us -> 1310 us (0.963)
  waiting for transfers between devices: 1290 us -> 1220 us
  blocking collectives: 0 us -> 26 us
    all_gather x1 -> x0, waiting for transfers between devices: 85.5 us -> none  [shards(): lax.all_gather(attended, 'col', axis=0, tiled=True)]
    all_to_all x0 -> x1, blocking collectives: none -> 26 us  [shards(): lax.all_to_all(jnp.stack([attended] * lax.axis_size('col')), 'col', 0, 0)]
  transfers between devices with their start and end apart: 7 -> 6, of which waited for: 7 -> 6; matrix products, arithmetic and copies ran while one was open for 1% -> 1% of each run, Pallas kernels for 0% -> 0%
where the time goes in v1:
time: 1310 us
  waiting for transfers between devices  1220 us (93%)
  blocking collectives  26 us (2%)
  starting transfers between devices  21.8 us (2%)
  matrix products  15.3 us (1%)
  between operations  13.3 us (1%)
    all_gather x1, waiting for transfers between devices, shards(): lax.all_gather(keyval_block.astype(jnp.bfloat16), ('row', 'col'), axis=0,...  693 us
    reduce_scatter x1, waiting for transfers between devices, shards(): lax.psum_scatter(query_part, 'col', scatter_dimension=1, tiled=True)  221 us
    reduce_scatter x1, waiting for transfers between devices, shards(): lax.psum_scatter(keyval_part, 'col', scatter_dimension=0, tiled=True)  207 us
    reduce_scatter x1, waiting for transfers between devices, shards(): lax.psum_scatter(partial_out.astype(jnp.bfloat16), 'row', scatter_dimensi...  46.4 us
    all_gather x1, waiting for transfers between devices, shards(): gathered = lax.all_gather(tokens, 'row', axis=0, tiled=True)  42.1 us
  transfers between devices with their start and end apart: 6, of which 6 were waited for; matrix products, arithmetic and copies ran while one was open for 1% of the time, Pallas kernels for 0%

profile of v1, /device:TPU:6, one launch (start us, length us, event | category | flops | bytes accessed | tf_op | source)
XLA Modules:
  0.0 1313.3 jit_solution(13301709037168163246)
XLA Ops:
  7.3 42.1 %all-gather.3.cloned.1.call-done = bf16[1024,512]{1,0:T(8,128)(2,1)} async-done(((bf16[128,512]{1,0:T(8,128)(2,1)}), bf16[1024,512]{1,0:T(8,128)(2,1)}) %all-gather.3.cloned.1.call-update) | async-done | bytes 1048592 | tf_op jit(solution)/shard_map/all_gather | solution.py:33
  49.4 2.6 fusion.45
  52.1 206.8 %reduce-scatter.4.cloned.1.call-done = f32[32,128]{1,0:T(8,128)} async-done(((f32[1024,128]{1,0:T(8,128)}), f32[32,128]{1,0:T(8,128)}) %reduce-scatter.4.cloned.1.call-update) | async-done | bytes 16400 | tf_op jit(solution)/shard_map/reduce_scatter | solution.py:43
  258.9 1.3 convert_element_type.55
  260.3 3.3 fusion.46
  263.9 1.9 multiply_cosine_fusion
  265.7 693.1 %all-gather.5.cloned.1.call-done = bf16[8192,128]{1,0:T(8,128)(2,1)} async-done(((bf16[32,128]{1,0:T(8,128)(2,1)}), bf16[8192,128]{1,0:T(8,128)(2,1)}) %all-gather.5.cloned.1.call-update) | async-done | bytes 2097168 | tf_op jit(solution)/shard_map/all_gather | solution.py:45
  958.8 2.9 fusion.4
  961.8 1.8 subtract_convert_fusion
  963.6 2.5 pad_maximum_fusion
  966.1 221.0 %reduce-scatter.6.cloned.1.call-done = f32[1024,32]{0,1:T(8,128)} async-done(((f32[1024,1024]{0,1:T(8,128)}), f32[1024,32]{0,1:T(8,128)}) %reduce-scatter.6.cloned.1.call-update) | async-done | bytes 131088 | tf_op jit(solution)/shard_map/reduce_scatter | solution.py:42
  1187.0 1.9 copy.22
  1188.9 1.9 reshape.300
  1190.9 21.4 %all-to-all-start = ((f32[32,1,1024]{2,1,0:T(1,128)}), f32[32,1,1024]{2,1,0:T(1,128)S(1)}, u32[]{:S(2)}, u32[]{:S(2)}) async-start(f32[32,1,1024]{2,1,0:T(1,128)} %reshape.300), calls=%async_computation.2 | async-start | bytes 262144 | tf_op jit(solution)/shard_map/all_to_all | solution.py:44
  1212.5 2.7 convolution_convert_fusion
  1215.2 8.4 all-to-all-done
  1224.1 0.9 reduce
  1225.1 1.0 reshape.301
  1226.1 2.2 copy.15
  1228.3 1.2 reshape.296
  1229.6 1.0 fusion.44
  1232.1 26.0 %all_to_all.21 = bf16[32,32,1024]{2,1,0:T(8,128)(2,1)S(1)} all-to-all(bf16[32,32,1024]{2,1,0:T(8,128)(2,1)S(1)} %stack.3), channel_id=1, replica_groups=mesh['row'=8,'col'=32] {'col'}, dimensions={0} | all-to-all | bytes 4194304 | tf_op jit(solution)/shard_map/all_to_all | solution.py:83
  1258.1 2.2 convolution_convert_fusion.1
  1260.4 46.4 %reduce-scatter.8.cloned.1.call-done = bf16[128,512]{1,0:T(8,128)(2,1)} async-done(((bf16[1024,512]{1,0:T(8,128)(2,1)}), bf16[128,512]{1,0:T(8,128)(2,1)}) %reduce-scatter.8.cloned.1.call-update) | async-done | bytes 131088 | tf_op jit(solution)/shard_map/reduce_scatter | solution.py:88
  (34 shorter events, 3.5 us)
Async XLA Ops:
  6.5 253.7 %copy-start = (bf16[512,1024]{1,0:T(8,128)(2,1)S(1)}, bf16[512,1024]{1,0:T(8,128)(2,1)}, u32[]{:S(2)}) copy-start(bf16[512,1024]{1,0:T(8,128)(2,1)} %param.5) | copy-start | bytes 3145732
  6.5 42.9 %all-gather.3.cloned.1.call-start = ((), (), s32[]{:S(2)}) async-start(), calls=%async_computation.5 | async-start | bytes 1179648 | tf_op jit(solution)/shard_map/all_gather | solution.py:33
  7.3 251.6 %reduce-scatter.4.cloned.1.call-start = ((), (), s32[]{:S(2)}) async-start(), calls=%async_computation.6 | async-start | bytes 540672 | tf_op jit(solution)/shard_map/reduce_scatter | solution.py:43
  49.4 210.8 %copy-start.4 = (bf16[1024,512]{1,0:T(8,128)(2,1)S(1)}, bf16[1024,512]{1,0:T(8,128)(2,1)}, u32[]{:S(2)}) copy-start(bf16[1024,512]{1,0:T(8,128)(2,1)} %all-gather.3.cloned.1.call-done) | copy-start | bytes 3145732
  52.0 906.8 %all-gather.5.cloned.1.call-start = ((), (), s32[]{:S(2)}) async-start(), calls=%async_computation.7 | async-start | bytes 2105344 | tf_op jit(solution)/shard_map/all_gather | solution.py:45
  260.2 926.8 %reduce-scatter.6.cloned.1.call-start = ((), (), s32[]{:S(2)}) async-start(), calls=%async_computation.8 | async-start | bytes 4325376 | tf_op jit(solution)/shard_map/reduce_scatter | solution.py:42
  963.6 249.0 %copy-start.1 = (bf16[8192,128]{1,0:T(8,128)(2,1)S(1)}, bf16[8192,128]{1,0:T(8,128)(2,1)}, u32[]{:S(2)}) copy-start(bf16[8192,128]{1,0:T(8,128)(2,1)} %all-gather.5.cloned.1.call-done) | copy-start | bytes 6291460
  1190.9 32.7 %all-to-all-start = ((f32[32,1,1024]{2,1,0:T(1,128)}), f32[32,1,1024]{2,1,0:T(1,128)S(1)}, u32[]{:S(2)}, u32[]{:S(2)}) async-start(f32[32,1,1024]{2,1,0:T(1,128)} %reshape.300), calls=%async_computation.2 | async-start | bytes 262144 | tf_op jit(solution)/shard_map/all_to_all | solution.py:44
  1212.3 94.5 %reduce-scatter.8.cloned.1.call-start = ((), (), s32[]{:S(2)}) async-start(), calls=%async_computation.9 | async-start | bytes 1179648 | tf_op jit(solution)/shard_map/reduce_scatter | solution.py:88
  1215.2 14.4 %copy-start.2 = (bf16[8,1024,128]{2,0,1:T(8,128)(2,1)S(1)}, bf16[8,1024,128]{2,0,1:T(8,128)(2,1)}, u32[]{:S(2)}) copy-start(bf16[8,1024,128]{2,0,1:T(8,128)(2,1)} %pad_maximum_fusion) | copy-start | bytes 6291460
  1229.6 1.6 copy-start.3
  1232.1 26.0 %copy-start.5 = (bf16[1024,512]{1,0:T(8,128)(2,1)S(1)}, bf16[1024,512]{1,0:T(8,128)(2,1)}, u32[]{:S(2)}) copy-start(bf16[1024,512]{1,0:T(8,128)(2,1)} %param.7) | copy-start | bytes 3145732
Sparse Core Ops, SparseCore 0:
  9.1 40.2 all-gather.2
  52.1 206.6 reduce-scatter.3
  260.9 697.8 all-gather.4
  961.4 225.6 reduce-scatter.5
  1260.5 46.2 reduce-scatter.7
